TPU v7x, 32 devices: a whole 2x2x4 slice. The times are simulated.
32 devices in a mesh: group: 2 (over x), inst: 2 (over core), tp: 8 (over z, y).
Axes of the slice: x: 2, y: 2, z: 4, core: 2. Of those that a mesh axis runs over, the one named last changes fastest.
Arguments:
- hidden: bfloat16 [2, 256, 8192], P(None, ('group', 'inst', 'tp')), parts along dimension 1, may hold values from -140 to 140
- norm_gain: float32 [2, 8192], replicated, may hold values from 0.1 to 1.9
- kv_weight: bfloat16 [2, 2048, 8192], P(None, 'tp'), may hold values from -0.0625 to 0.0625
- kv_bias: float32 [2, 2048], P(None, 'tp'), may hold values from -3 to 3
- block_request: int32 [32], P(('group', 'inst', 'tp')), parts along dimension 0, may hold values from 0 to 3, never falling along the last dimension, each value on 1 to 8 neighbouring positions
- request_dest: int32 [8], P('group'), parts along dimension 0, may hold values from 0 to 1
- block_slot: int32 [32], P(('group', 'inst', 'tp')), parts along dimension 0, may hold values from 0 to 15, each once
- positions: int32 [256], P(('group', 'inst', 'tp')), parts along dimension 0, may hold values from 0 to 32767
Outputs:
- kv_cache: bfloat16 [2, 64, 8, 2048], P(None, ('group', 'inst'), 'tp'), parts along dimension 1
There are 2 independent parts, one for each index of `group`. A program takes and returns all parts, laid end to end along the dimension named above; an argument that names none is the same for every part. Nothing has to cross between parts.
All inputs are finite; a program needn't handle non-finite values.
Results may differ from a plain program's by a relative error of at most 0.0047.
Values may be sent and summed in bfloat16 or wider, within the bound.
A program may use at most 64 MiB of HBM per device.

v0:
```python
import math

import jax
import jax.numpy as jnp
from jax import lax
from jax.sharding import PartitionSpec as P

HD = 128


EPSILON = 1e-06
ROPE_BASE = 1000000.0


def rotary_parts(columns):
    freq_idx = columns % HD // 2
    inv_freq = jnp.exp(-(2.0 * freq_idx.astype(jnp.float32) / HD) * math.log(ROPE_BASE))
    is_key = columns % (2 * HD) < HD
    return (inv_freq, is_key)


def project(hidden_rows, gain_row, weight, bias_row, places, inv_freq, is_key):
    values_f = hidden_rows.astype(jnp.float32)
    inv_rms = lax.rsqrt(jnp.mean(values_f * values_f, axis=-1, keepdims=True) + EPSILON)
    normed = (values_f * inv_rms * gain_row).astype(jnp.bfloat16)
    projected = (
        lax.dot_general(
            normed, weight, (((1,), (1,)), ((), ())), preferred_element_type=jnp.float32
        )
        + bias_row
    )
    angles = places[:, None].astype(jnp.float32) * inv_freq[None, :]
    paired = projected.reshape(projected.shape[0], -1, 2)
    partner = jnp.stack([-paired[:, :, 1], paired[:, :, 0]], axis=-1).reshape(projected.shape)
    turned = projected * jnp.cos(angles) + partner * jnp.sin(angles)
    return jnp.where(is_key[None, :], turned, projected).astype(jnp.bfloat16)


def write_pages(slots, pages, slot_count):
    target = jnp.where(slots >= 0, slots, slot_count)
    empty = jnp.zeros((slot_count,) + pages.shape[1:], jnp.bfloat16)
    return empty.at[target].set(pages, mode="drop")


def body(hidden, norm_gain, kv_weight, kv_bias, block_request, request_dest, block_slot, positions):
    layer_count = hidden.shape[0]
    row_count = hidden.shape[1]
    model_dim = hidden.shape[2]
    page_count = block_request.shape[0]
    page_len = row_count // page_count
    col_width = kv_weight.shape[1]
    page_width = page_len * col_width
    inst_count = lax.axis_size("inst")
    team_size = lax.axis_size("tp")
    slot_count = inst_count * team_size * page_count
    columns = lax.axis_index("tp") * col_width + jnp.arange(col_width, dtype=jnp.int32)
    inv_freq, is_key = rotary_parts(columns)
    matched = block_request[:, None] == jnp.arange(request_dest.shape[0], dtype=jnp.int32)[None, :]
    block_dest = jnp.sum(jnp.where(matched, request_dest[None, :], 0), axis=1)
    owners = jnp.arange(inst_count, dtype=jnp.int32)
    caches = []
    row_dest = jnp.repeat(block_dest, page_len)
    chosen = row_dest[None, :] == owners[:, None]
    outgoing = jnp.where(chosen[:, None, :, None], hidden[None], jnp.zeros((), hidden.dtype))
    slot_out = jnp.where(block_dest[None, :] == owners[:, None], block_slot[None, :], -1)
    place_out = jnp.broadcast_to(positions[None, :], (inst_count, row_count))
    got_rows, got_slots, got_places = (
        lax.all_to_all(outgoing, "inst", split_axis=0, concat_axis=0, tiled=True),
        lax.all_to_all(slot_out, "inst", split_axis=0, concat_axis=0, tiled=True),
        lax.all_to_all(place_out, "inst", split_axis=0, concat_axis=0, tiled=True),
    )
    team_rows, team_slots, team_places = (
        lax.all_gather(got_rows, "tp", axis=2, tiled=True),
        lax.all_gather(got_slots, "tp", axis=1, tiled=True),
        lax.all_gather(got_places, "tp", axis=1, tiled=True),
    )
    flat_slots = team_slots.reshape(-1)
    flat_places = team_places.reshape(-1)
    for layer_idx in range(layer_count):
        rotated = project(
            team_rows[:, layer_idx].reshape(-1, model_dim),
            norm_gain[layer_idx],
            kv_weight[layer_idx],
            kv_bias[layer_idx],
            flat_places,
            inv_freq,
            is_key,
        )
        caches.append(write_pages(flat_slots, rotated.reshape(-1, 1, page_width), slot_count))
    return jnp.stack(caches)


def solution(mesh):
    placed = (
        P(None, ("group", "inst", "tp"), None),
        P(),
        P(None, "tp", None),
        P(None, "tp"),
        P(("group", "inst", "tp")),
        P("group"),
        P(("group", "inst", "tp")),
        P(("group", "inst", "tp")),
    )
    return jax.shard_map(
        body,
        mesh=mesh,
        in_specs=placed,
        out_specs=P(None, ("group", "inst"), "tp", None),
        check_vma=False,
    )
```

profile of v0, /device:TPU:0, one launch (start us, length us, event | category | flops | bytes accessed | tf_op | source)
XLA Modules:
  0.0 114.3 jit_solution(14172046476686759991)
XLA Ops:
  6.5 0.0 all-gather.4.cloned.1.call-start
  7.2 1.3 %fusion.34 = s32[]{:T(128)} fusion(s32[4]{0:T(128)} %param.13, s32[]{:T(128)} %bitcast.32), kind=kLoop, calls=%fused_computation.61 | loop fusion | flops 11 | bytes 24 | tf_op jit(solution)/shard_map/reduce_sum | solution.py:59
  8.5 0.6 iota_compare_fusion
  9.0 1.1 broadcast_select_fusion
  10.1 4.9 %all_to_all.23 = bf16[2,2,8,8192]{3,2,1,0:T(8,128)(2,1)} all-to-all(bf16[2,2,8,8192]{3,2,1,0:T(8,128)(2,1)S(1)} %broadcast_select_fusion), channel_id=1, replica_groups=mesh['group'=2,'inst'=2,'tp'=8] {'inst'}, dimensions={0} | all-to-all | bytes 1048576 | tf_op jit(solution)/shard_map/all_to_all | solution.py:68
  15.0 0.0 all-gather.4.cloned.1.call-update
  15.7 0.6 compare_select_fusion
  16.2 3.7 %all_to_all.24 = s32[2,1,1]{1,2,0:T(1,128)S(1)} all-to-all(s32[2,1,1]{1,2,0:T(1,128)S(1)} %compare_select_fusion), channel_id=1, replica_groups=mesh['group'=2,'inst'=2,'tp'=8] {'inst'}, dimensions={0} | all-to-all | bytes 16 | tf_op jit(solution)/shard_map/all_to_all | solution.py:69
  19.9 0.1 copy.29
  20.0 1.2 %broadcast_in_dim.86 = s32[2,1,8]{2,1,0:T(1,128)} broadcast(s32[8]{0:T(128)} %param.15), dimensions={2} | broadcast | bytes 96 | tf_op jit(solution)/shard_map/broadcast_in_dim | solution.py:66
  21.2 3.2 %all-to-all-start.2 = ((s32[2,1,8]{2,1,0:T(1,128)}), s32[2,1,8]{2,1,0:T(1,128)S(1)}, u32[]{:S(2)}, u32[]{:S(2)}) async-start(s32[2,1,8]{2,1,0:T(1,128)} %broadcast_in_dim.86), calls=%async_computation.2 | async-start | bytes 2048 | tf_op jit(solution)/shard_map/all_to_all | solution.py:70
  24.4 22.4 %all-gather = s32[2,8,1]{0,2,1:T(1,128)S(1)} all-gather(s32[2,1,1]{0,2,1:T(1,128)S(1)} %copy.29), channel_id=2, replica_groups=mesh['group'=2,'inst'=2,'tp'=8] {'tp'}, dimensions={1}, use_global_device_ids=true | all-gather | bytes 72 | tf_op jit(solution)/shard_map/all_gather | solution.py:74
  46.8 0.0 all-to-all-done.2
  46.8 0.1 copy.31
  46.9 30.9 %all-gather.1 = s32[2,1,64]{0,1,2:T(1,128)S(1)} all-gather(s32[2,1,8]{0,1,2:T(1,128)S(1)} %copy.31), channel_id=3, replica_groups=mesh['group'=2,'inst'=2,'tp'=8] {'tp'}, dimensions={2}, use_global_device_ids=true | all-gather | bytes 576 | tf_op jit(solution)/shard_map/all_gather | solution.py:75
  77.8 0.1 copy.32
  77.9 0.1 convert_element_type.51
  77.9 0.1 copy.30
  78.0 0.1 reshape.196
  78.2 0.8 fusion.37
  78.9 1.0 fusion.36
  79.9 11.8 %all-gather.4.cloned.1.call-done = bf16[2,2,64,8192]{3,2,1,0:T(8,128)(2,1)} async-done(((bf16[2,2,8,8192]{3,2,1,0:T(8,128)(2,1)}), bf16[2,2,64,8192]{3,2,1,0:T(8,128)(2,1)}) %all-gather.4.cloned.1.call-update) | async-done | bytes 4194320 | tf_op jit(solution)/shard_map/all_gather | solution.py:73
  91.7 0.0 copy-start
  91.7 3.3 %fusion = (f32[2,64]{1,0:T(2,128)S(1)}, f32[2,64]{1,0:T(2,128)S(1)}) fusion(bf16[2,2,64,8192]{3,2,1,0:T(8,128)(2,1)} %all-gather.4.cloned.1.call-done), kind=kLoop, calls=%fused_computation.6 | loop fusion | flops 6291200 | bytes 4195328 | tf_op jit(solution)/shard_map/reduce_sum | solution.py:24
  95.0 0.1 copy-done
  95.1 0.0 copy-start.1
  95.1 1.2 %fusion.2 = (bf16[2,1,64,8192]{3,2,1,0:T(8,128)(2,1)S(1)}, bf16[2,1,64,8192]{3,2,1,0:T(8,128)(2,1)S(1)}) fusion(f32[8192]{0:T(1024)S(1)} %bitcast.42, f32[2,64]{1,0:T(2,128)S(1)} %get-tuple-element.20, bf16[2,2,64,8192]{3,2,1,0:T(8,128)(2,1)S(1)} %copy-done, f32[8192]{0:T(1024)S(1)} %bitcast.43, f32[2,64]{1,0:T(2,128)S(1)} %get-tuple-element.19), kind=kLoop, calls=%fused_computation.8 | loop fusion | flops 8388608 | bytes 8455168 | tf_op jit(solution)/shard_map/convert_element_type | solution.py:25
  96.3 2.2 %copy-done.1 = bf16[2,256,8192]{2,1,0:T(8,128)(2,1)S(1)} copy-done((bf16[2,256,8192]{2,1,0:T(8,128)(2,1)S(1)}, bf16[2,256,8192]{2,1,0:T(8,128)(2,1)}, u32[]{:S(2)}) %copy-start.1) | copy-done | bytes 8388632
  98.5 1.5 %fusion.15 = f32[128,256]{1,0:T(8,128)S(1)} fusion(bf16[128,8192]{1,0:T(8,128)(2,1)S(1)} %bitcast.35, bf16[2,256,8192]{2,1,0:T(8,128)(2,1)S(1)} %copy-done.1, f32[256]{0:T(256)S(1)} %bitcast.45), kind=kOutput, calls=%fused_computation.19 | convolution fusion | flops 536903680 | bytes 6423552 | tf_op jit(solution)/shard_map/dot_general | solution.py:27
  100.1 0.1 copy.35
  100.2 0.1 slice_negate_fusion
  100.3 0.1 pad_maximum_fusion.1
  100.4 0.1 copy.36
  100.5 3.7 %fusion.12 = f32[128,256]{1,0:T(8,128)S(1)} fusion(bf16[128,8192]{1,0:T(8,128)(2,1)S(1)} %bitcast.34, bf16[2,256,8192]{2,1,0:T(8,128)(2,1)} %param.10, f32[256]{0:T(256)S(1)} %bitcast.44), kind=kOutput, calls=%fused_computation.18 | convolution fusion | flops 536903680 | bytes 6423552 | tf_op jit(solution)/shard_map/dot_general | solution.py:27
  104.2 0.1 copy.33
  104.3 0.1 slice_negate_fusion.1
  104.4 0.1 pad_maximum_fusion
  104.6 0.1 copy.34
  104.7 0.6 fusion.24
  105.3 0.7 scatter_custom_fusion
  106.1 0.7 scatter_custom_fusion.1
  106.8 0.7 pad_maximum_fusion.2
  (7 shorter events, 0.1 us)
Async XLA Ops:
  6.5 85.2 %all-gather.4.cloned.1.call-start = ((), (), s32[]{:S(2)}) async-start(), calls=%async_computation.3 | async-start | bytes 4718592 | tf_op jit(solution)/shard_map/all_gather | solution.py:73
  21.2 25.6 %all-to-all-start.2 = ((s32[2,1,8]{2,1,0:T(1,128)}), s32[2,1,8]{2,1,0:T(1,128)S(1)}, u32[]{:S(2)}, u32[]{:S(2)}) async-start(s32[2,1,8]{2,1,0:T(1,128)} %broadcast_in_dim.86), calls=%async_computation.2 | async-start | bytes 2048 | tf_op jit(solution)/shard_map/all_to_all | solution.py:70
  91.7 3.5 %copy-start = (bf16[2,2,64,8192]{3,2,1,0:T(8,128)(2,1)S(1)}, bf16[2,2,64,8192]{3,2,1,0:T(8,128)(2,1)}, u32[]{:S(2)}) copy-start(bf16[2,2,64,8192]{3,2,1,0:T(8,128)(2,1)} %all-gather.4.cloned.1.call-done) | copy-start | bytes 12582916
  95.1 3.4 %copy-start.1 = (bf16[2,256,8192]{2,1,0:T(8,128)(2,1)S(1)}, bf16[2,256,8192]{2,1,0:T(8,128)(2,1)}, u32[]{:S(2)}) copy-start(bf16[2,256,8192]{2,1,0:T(8,128)(2,1)} %param.10) | copy-start | bytes 25165828
Sparse Core Ops, SparseCore 0:
  15.1 76.4 all-gather.3
where the time goes:
time: 115 us; the launch traced here: 114 us
  blocking collectives  61.8 us (54%)
  between operations  14.9 us (13%)
  waiting for transfers between devices  11.8 us (10%)
  other arithmetic  9.74 us (8%)
  local copies, waits for them, and re-layouts  7.63 us (7%)
  matrix products  5.25 us (5%)
  starting transfers between devices  3.2 us (3%)
    all_gather x1, blocking collectives, body(): lax.all_gather(got_places, 'tp', axis=1, tiled=True)  30.9 us
    all_gather x1, blocking collectives, body(): lax.all_gather(got_slots, 'tp', axis=1, tiled=True)  22.4 us
    all_gather x1, waiting for transfers between devices, body(): lax.all_gather(got_rows, 'tp', axis=2, tiled=True)  11.8 us
    dot_general x2, matrix products, project(): lax.dot_general(normed, weight, (((1,), (1,)), ((), ())), preferred_eleme...  5.25 us
    all_to_all x1, blocking collectives, body(): lax.all_to_all(outgoing, 'inst', split_axis=0, concat_axis=0, tiled=True)  4.89 us
    all_to_all x1, blocking collectives, body(): lax.all_to_all(slot_out, 'inst', split_axis=0, concat_axis=0, tiled=True)  3.66 us
    reduce_sum x1, other arithmetic, project(): jnp.mean(values_f * values_f, axis=-1, keepdims=True) + EPSILON  3.29 us
    all_to_all x1, starting transfers between devices, body(): lax.all_to_all(place_out, 'inst', split_axis=0, concat_axis=0, tiled=True)  3.19 us
  transfers between devices with their start and end apart: 2, of which 1 were waited for; matrix products, arithmetic and copies ran while one was open for 4% of the time, Pallas kernels for 0%

commit v1 on v0

v1 whole, which is shorter than its diff:
```python
import functools
import math

import jax
import jax.numpy as jnp
from jax import lax
from jax.experimental import pallas as pl
from jax.experimental.pallas import tpu as pltpu
from jax.sharding import PartitionSpec as P

HD = 128
EPSILON = 1e-06
ROPE_BASE = 1000000.0
LOOKAHEAD = 3
MESH = pl.DeviceIdType.MESH
Y, UP, DOWN = 0, 1, 2


def kernel(
    team, chunks, page_len, page_count, slots,
    request_ref, dest_ref, slot_ref, place_ref,
    hidden_hbm, gain_hbm, weight_hbm, bias_hbm,
    out_ref,
    hidden, gain, weight, bias, rows, meta, far_code, total, turned, cos_ref, sin_ref, pick,
    load_sem, send_sem, recv_sem, meta_send, meta_recv, pair_send, pair_recv,
):
    layers, row_count, model_dim = hidden.shape
    width = weight.shape[1]
    wide = total.shape[2]
    depth = model_dim // chunks
    line = team // 2
    inst = lax.axis_index("inst")
    me = lax.axis_index("tp")
    z = me // 2
    y = me % 2
    peer = (me + 1 - 2 * y, me + 2, me - 2)
    has_up = z < line - 1
    has_down = z > 0

    loads = [
        pltpu.make_async_copy(hidden_hbm, hidden, load_sem.at[0]),
        pltpu.make_async_copy(gain_hbm, gain, load_sem.at[1]),
        pltpu.make_async_copy(bias_hbm, bias, load_sem.at[2]),
        pltpu.make_async_copy(weight_hbm, weight, load_sem.at[3]),
    ]
    for load in loads:
        load.start()

    barrier = pltpu.get_barrier_semaphore()
    pl.semaphore_signal(barrier, inc=1, device_id={"inst": 1 - inst}, device_id_type=MESH)
    pl.semaphore_signal(barrier, inc=1, device_id={"tp": peer[Y]}, device_id_type=MESH)

    @pl.when(has_up)
    def _():
        pl.semaphore_signal(barrier, inc=1, device_id={"tp": peer[UP]}, device_id_type=MESH)

    @pl.when(has_down)
    def _():
        pl.semaphore_signal(barrier, inc=1, device_id={"tp": peer[DOWN]}, device_id_type=MESH)

    sub = lax.broadcasted_iota(jnp.int32, (row_count, 128), 0)
    place = jnp.zeros((row_count, 128), jnp.int32)
    code = jnp.zeros((row_count, 128), jnp.int32)
    for r in range(row_count):
        place = jnp.where(sub == r, place_ref[r], place)
    for b in range(page_count):
        dest = jnp.int32(0)
        for q in range(dest_ref.shape[0]):
            dest = dest + jnp.where(request_ref[b] == q, dest_ref[q], 0)
        code = jnp.where(sub // page_len == b, dest * slots + slot_ref[b], code)
    meta[me, 0] = place
    meta[me, 1] = code

    loads[0].wait()
    loads[1].wait()
    inv_rms = []
    for layer in range(layers):
        square = jnp.zeros((row_count, 128), jnp.float32)
        for j in range(model_dim // 128):
            values = hidden[layer, :, j * 128:(j + 1) * 128].astype(jnp.float32)
            square = square + values * values
        mean = jnp.sum(square, axis=1, keepdims=True) * (1.0 / model_dim)
        inv_rms.append(lax.rsqrt(mean + EPSILON))

    pl.semaphore_wait(barrier, 2 + has_up.astype(jnp.int32) + has_down.astype(jnp.int32))

    def copies(c, block, way):
        made = [
            pltpu.make_async_remote_copy(
                src_ref=rows.at[c, block], dst_ref=rows.at[c, block],
                send_sem=send_sem.at[way, c, block], recv_sem=recv_sem.at[c, block],
                device_id={"tp": peer[way]}, device_id_type=MESH,
            )
        ]
        if c == 0:
            made.append(
                pltpu.make_async_remote_copy(
                    src_ref=meta.at[block], dst_ref=meta.at[block],
                    send_sem=meta_send.at[way, block], recv_sem=meta_recv.at[block],
                    device_id={"tp": peer[way]}, device_id_type=MESH,
                )
            )
        return made

    def send(c, block, way):
        for copy in copies(c, block, way):
            copy.start()

    def receive(c, block):
        for copy in copies(c, block, Y):
            copy.wait_recv()

    def send_own(c):
        span = slice(c * depth, (c + 1) * depth)
        normed = [
            hidden[layer, :, span].astype(jnp.float32) * inv_rms[layer] * gain[layer:layer + 1, span]
            for layer in range(layers)
        ]
        rows[c, me] = jnp.concatenate(normed, axis=0).astype(jnp.bfloat16)
        send(c, me, Y)
        pl.when(has_up)(lambda: send(c, me, UP))
        pl.when(has_down)(lambda: send(c, me, DOWN))

    def forward(c, step):
        low, high = me - 2 * step, me + 2 * step

        @pl.when(z >= step)
        def _():
            receive(c, low)
            send(c, low, Y)
            pl.when(has_up)(lambda: send(c, low, UP))

        @pl.when(z + step < line)
        def _():
            receive(c, high)
            send(c, high, Y)
            pl.when(has_down)(lambda: send(c, high, DOWN))

    tokens = team * row_count
    places = page_len * slots

    pair_code = pltpu.make_async_remote_copy(
        src_ref=meta, dst_ref=far_code, send_sem=pair_send.at[0], recv_sem=pair_recv.at[0],
        device_id={"inst": 1 - inst}, device_id_type=MESH,
    )

    def tables():
        position = meta[:, 0].reshape(tokens, 128).astype(jnp.float32)
        for g in range(wide // 128):
            if width % (2 * HD) == 0 and g % 2:
                continue
            column = me * width + g * 128 + lax.broadcasted_iota(jnp.int32, (1, 128), 1)
            freq = (column % HD // 2).astype(jnp.float32)
            angle = position * jnp.exp(-(2.0 * freq / HD) * math.log(ROPE_BASE))
            is_key = column % (2 * HD) < HD
            lanes = slice(g * 128, (g + 1) * 128)
            cos_ref[:, lanes] = jnp.where(is_key, jnp.cos(angle), 1.0)
            sine = jnp.where(is_key, jnp.sin(angle), 0.0)
            sin_ref[:, lanes] = jnp.where(column % 2 == 0, -sine, sine)

    def picks(side, source):
        code = source[:, 1].reshape(tokens, 128)[:, 0:1]
        spot = lax.broadcasted_iota(jnp.int32, (tokens, places), 1)
        token = lax.broadcasted_iota(jnp.int32, (tokens, places), 0)
        hit = (code == inst * slots + spot % slots) & (token % page_len == spot // slots)
        pick[side] = jnp.where(hit, 1.0, 0.0).T.astype(jnp.bfloat16)

    def multiply(c):
        block = rows[c].reshape(team * layers * row_count, depth)
        for layer in range(layers):
            part = lax.dot_general(
                block, weight[layer, :, c * depth:(c + 1) * depth],
                (((1,), (1,)), ((), ())), preferred_element_type=jnp.float32,
            )
            if c == 0:
                total[layer, :, :width] = part
            else:
                total[layer, :, :width] += part

    if wide != width:
        total[...] = jnp.zeros_like(total)
    for c in range(min(LOOKAHEAD, chunks)):
        send_own(c)
    for wave in range(chunks + line):
        if wave + LOOKAHEAD < chunks:
            send_own(wave + LOOKAHEAD)
        for step in range(1, line):
            if 0 <= wave - step < chunks:
                forward(wave - step, step)
        c = wave - line
        if 0 <= c < chunks:
            for far in range(line):
                receive(c, 2 * far + 1 - y)
            if c == 0:
                pair_code.start()
                loads[2].wait()
                loads[3].wait()
                tables()
                picks(0, meta)
            multiply(c)
    pair_code.wait_recv()
    picks(1, far_code)

    lane = lax.broadcasted_iota(jnp.int32, (1, 128), 1)
    for layer in range(layers):
        acc = total[layer].reshape(team, layers * row_count, wide)
        acc = acc[:, layer * row_count:(layer + 1) * row_count].reshape(tokens, wide)
        for g in range(wide // 128):
            start, end = g * 128, min((g + 1) * 128, width)
            value = acc[:, g * 128:(g + 1) * 128]
            shift = bias[layer:layer + 1, start:end]
            if end - start < 128:
                shift = jnp.pad(shift, ((0, 0), (0, 128 - (end - start))))
            value = value + shift
            if not (width % (2 * HD) == 0 and g % 2):
                after = pltpu.roll(value, 127, 1)
                before = pltpu.roll(value, 1, 1)
                partner = jnp.where(lane % 2 == 0, after, before)
                value = value * cos_ref[:, start:start + 128] + partner * sin_ref[:, start:start + 128]
            turned[0, layer, :, g * 128:(g + 1) * 128] = value.astype(jnp.bfloat16)

    swap = pltpu.make_async_remote_copy(
        src_ref=turned.at[0], dst_ref=turned.at[1], send_sem=pair_send.at[1], recv_sem=pair_recv.at[1],
        device_id={"inst": 1 - inst}, device_id_type=MESH,
    )
    swap.start()
    near = [
        jnp.dot(pick[0], turned[0, layer], preferred_element_type=jnp.float32) for layer in range(layers)
    ]
    swap.wait_recv()
    for layer in range(layers):
        paged = near[layer] + jnp.dot(pick[1], turned[1, layer], preferred_element_type=jnp.float32)
        paged = paged.astype(jnp.bfloat16)
        for r in range(page_len):
            page_rows = paged[r * slots:(r + 1) * slots]
            if out_ref.ndim == 3:
                out_ref[layer, :, r * width:(r + 1) * width] = page_rows
            else:
                out_ref[layer, r] = page_rows

    def sent(c, block, way):
        for copy in copies(c, block, way):
            copy.wait_send()

    pair_code.wait_send()
    swap.wait_send()
    for c in range(chunks):
        sent(c, me, Y)
        pl.when(has_up)(functools.partial(sent, c, me, UP))
        pl.when(has_down)(functools.partial(sent, c, me, DOWN))
        for step in range(1, line):
            low, high = me - 2 * step, me + 2 * step

            @pl.when(z >= step)
            def _():
                sent(c, low, Y)
                pl.when(has_up)(functools.partial(sent, c, low, UP))

            @pl.when(z + step < line)
            def _():
                sent(c, high, Y)
                pl.when(has_down)(functools.partial(sent, c, high, DOWN))


def body(hidden, norm_gain, kv_weight, kv_bias, block_request, request_dest, block_slot, positions):
    layers, row_count, model_dim = hidden.shape
    page_count = block_request.shape[0]
    page_len = row_count // page_count
    width = kv_weight.shape[1]
    inst_count = lax.axis_size("inst")
    team = lax.axis_size("tp")
    slots = inst_count * team * page_count
    wide = -(-width // 128) * 128
    chunks = max(1, 64 // team)
    depth = model_dim // chunks
    tokens = team * row_count
    line = team // 2
    if wide == width:
        shape = (layers, slots, page_len * width)
    else:
        shape = (layers, page_len, slots, wide)
    smem = pl.BlockSpec(memory_space=pltpu.SMEM)
    anywhere = pl.BlockSpec(memory_space=pl.ANY)
    dma = pltpu.SemaphoreType.DMA
    out = pl.pallas_call(
        functools.partial(kernel, team, chunks, page_len, page_count, slots),
        out_shape=jax.ShapeDtypeStruct(shape, jnp.bfloat16),
        in_specs=[smem] * 4 + [anywhere] * 4,
        out_specs=pl.BlockSpec(memory_space=pltpu.VMEM),
        scratch_shapes=[
            pltpu.VMEM((layers, row_count, model_dim), jnp.bfloat16),
            pltpu.VMEM((layers, model_dim), jnp.float32),
            pltpu.VMEM((layers, width, model_dim), jnp.bfloat16),
            pltpu.VMEM((layers, width), jnp.float32),
            pltpu.VMEM((chunks, team, layers * row_count, depth), jnp.bfloat16),
            pltpu.VMEM((team, 2, row_count, 128), jnp.int32),
            pltpu.VMEM((team, 2, row_count, 128), jnp.int32),
            pltpu.VMEM((layers, team * layers * row_count, wide), jnp.float32),
            pltpu.VMEM((2, layers, tokens, wide), jnp.bfloat16),
            pltpu.VMEM((tokens, wide), jnp.float32),
            pltpu.VMEM((tokens, wide), jnp.float32),
            pltpu.VMEM((2, page_len * slots, tokens), jnp.bfloat16),
            dma((4,)),
            dma((3, chunks, team)),
            dma((chunks, team)),
            dma((3, team)),
            dma((team,)),
            dma((2,)),
            dma((2,)),
        ],
        compiler_params=pltpu.CompilerParams(
            collective_id=0, has_side_effects=True, vmem_limit_bytes=48 * 1024 * 1024
        ),
        cost_estimate=pl.CostEstimate(
            flops=4 * layers * tokens * width * model_dim,
            bytes_accessed=2 * layers * width * model_dim,
            transcendentals=0,
        ),
        name="restore",
    )(block_request, request_dest, block_slot, positions, hidden, norm_gain, kv_weight, kv_bias)
    if wide != width:
        out = out[..., :width].transpose(0, 2, 1, 3)
    return out.reshape(layers, slots, 1, page_len * width)


def solution(mesh):
    placed = (
        P(None, ("group", "inst", "tp"), None),
        P(),
        P(None, "tp", None),
        P(None, "tp"),
        P(("group", "inst", "tp")),
        P("group"),
        P(("group", "inst", "tp")),
        P(("group", "inst", "tp")),
    )
    return jax.shard_map(
        body,
        mesh=mesh,
        in_specs=placed,
        out_specs=P(None, ("group", "inst"), "tp", None),
        check_vma=False,
    )
```

time: 115 us -> 44.2 us (0.38)
  blocking collectives: 61.8 us -> 0 us
  Pallas kernels: 0 us -> 38.1 us
  between operations: 14.9 us -> 1.32 us
  waiting for transfers between devices: 11.8 us -> 0 us
  other arithmetic: 9.74 us -> 0 us
  matrix products: 5.25 us -> 0 us
  local copies, waits for them, and re-layouts: 7.63 us -> 4.43 us
  starting transfers between devices: 3.2 us -> 0 us
    all_gather x2 -> x0, blocking collectives: 53.3 us -> none  [the longest x1 30.9 us: body(): lax.all_gather(got_places, 'tp', axis=1, tiled=True)]
    pallas_call x0 -> x1, Pallas kernels: none -> 38.1 us  [body(): pl.pallas_call(functools.partial(kernel, team, chunks, page_len, page_cou...]
    all_gather x1 -> x0, waiting for transfers between devices: 11.8 us -> none  [body(): lax.all_gather(got_rows, 'tp', axis=2, tiled=True)]
    all_to_all x2 -> x0, blocking collectives: 8.55 us -> none  [the longest x1 4.89 us: body(): lax.all_to_all(outgoing, 'inst', split_axis=0, concat_axis=0, tiled=True)]
    dot_general x2 -> x0, matrix products: 5.25 us -> none  [project(): lax.dot_general(normed, weight, (((1,), (1,)), ((), ())), preferred_eleme...]
    reduce_sum x2 -> x0, other arithmetic: 4.58 us -> none  [the longest x1 3.29 us: project(): jnp.mean(values_f * values_f, axis=-1, keepdims=True) + EPSILON]
    all_to_all x1 -> x0, starting transfers between devices: 3.19 us -> none  [body(): lax.all_to_all(place_out, 'inst', split_axis=0, concat_axis=0, tiled=True)]
    unnamed x4 -> x11, local copies, waits for them, and re-layouts: 2.32 us -> 4.43 us
  transfers between devices with their start and end apart: 2 -> 0, of which waited for: 1 -> 0; matrix products, arithmetic and copies ran while one was open for 4% -> 0% of each run, Pallas kernels for 0% -> 0%
where the time goes in v1:
time: 44.2 us; the launch traced here: 43.8 us
  Pallas kernels  38.1 us (86%)
  local copies, waits for them, and re-layouts  4.43 us (10%)
  between operations  1.32 us (3%)
    pallas_call x1, Pallas kernels, body(): pl.pallas_call(functools.partial(kernel, team, chunks, page_len, page_cou...  38.1 us
    unnamed x11, local copies, waits for them, and re-layouts  4.43 us

profile of v1, /device:TPU:0, one launch (start us, length us, event | category | flops | bytes accessed | tf_op | source)
XLA Modules:
  0.0 43.8 jit_solution(1997237949294046811)
XLA Ops:
  1.3 0.0 copy-start
  1.3 0.9 %copy-done = bf16[2,8,8192]{2,1,0:T(8,128)(2,1)S(1)} copy-done((bf16[2,8,8192]{2,1,0:T(8,128)(2,1)S(1)}, bf16[2,8,8192]{2,1,0:T(8,128)(2,1)}, u32[]{:S(2)}) %copy-start) | copy-done | bytes 262168
  2.2 0.0 copy-start.1
  2.2 0.8 %copy-done.1 = f32[2,8192]{1,0:T(2,128)S(1)} copy-done((f32[2,8192]{1,0:T(2,128)S(1)}, f32[2,8192]{1,0:T(2,128)}, u32[]{:S(2)}) %copy-start.1) | copy-done | bytes 65560
  3.1 0.0 copy-start.2
  3.1 0.7 %copy-done.2 = f32[2,256]{1,0:T(2,128)S(1)} copy-done((f32[2,256]{1,0:T(2,128)S(1)}, f32[2,256]{1,0:T(2,128)}, u32[]{:S(2)}) %copy-start.2) | copy-done | bytes 2072
  3.8 0.0 copy-start.3
  3.8 0.7 %copy-done.3 = s32[4]{0:T(128)S(1)} copy-done((s32[4]{0:T(128)S(1)}, s32[4]{0:T(128)}, u32[]{:S(2)}) %copy-start.3) | copy-done | bytes 40
  4.4 0.0 copy-start.4
  4.4 0.7 %copy-done.4 = s32[8]{0:T(128)S(1)} copy-done((s32[8]{0:T(128)S(1)}, s32[8]{0:T(128)}, u32[]{:S(2)}) %copy-start.4) | copy-done | bytes 56
  5.1 38.1 %restore.1 = bf16[2,16,2048]{2,1,0:T(8,128)(2,1)S(1)} custom-call(s32[1]{0:T(128)S(6)} %copy.11.request_ref, s32[4]{0:T(128)S(1)} %copy-done.3, s32[1]{0:T(128)S(6)} %copy.12.slot_ref, s32[8]{0:T(128)S(1)} %copy-done.4, bf16[2,8,8192]{2,1,0:T(8,128)(2,1)S(1)} %copy-done, f32[2,8192]{1,0:T(2,128)S(1)} %copy-done.1, bf16[2,256,8192]{2,1,0:T(8,128)(2,1)} %weight_hbm.1, ...), custom_call_target="tpu_custom_call" | custom-call | flops 1073741824 | bytes 8388608 | tf_op jit(solution)/shard_map/restore/pallas_call | solution.py:285
  43.1 0.7 %copy.13 = bf16[2,16,1,2048]{3,1,2,0:T(8,128)(2,1)} copy(bf16[2,16,1,2048]{3,1,2,0:T(8,128)(2,1)S(1)} %bitcast.3) | data formatting | bytes 262144
Async XLA Ops:
  1.3 1.0 %copy-start = (bf16[2,8,8192]{2,1,0:T(8,128)(2,1)S(1)}, bf16[2,8,8192]{2,1,0:T(8,128)(2,1)}, u32[]{:S(2)}) copy-start(bf16[2,8,8192]{2,1,0:T(8,128)(2,1)} %hidden_hbm.1) | copy-start | bytes 786436
  2.2 0.8 %copy-start.1 = (f32[2,8192]{1,0:T(2,128)S(1)}, f32[2,8192]{1,0:T(2,128)}, u32[]{:S(2)}) copy-start(f32[2,8192]{1,0:T(2,128)} %gain_hbm.1) | copy-start | bytes 196612
  3.1 0.7 %copy-start.2 = (f32[2,256]{1,0:T(2,128)S(1)}, f32[2,256]{1,0:T(2,128)}, u32[]{:S(2)}) copy-start(f32[2,256]{1,0:T(2,128)} %bias_hbm.1) | copy-start | bytes 6148
  3.8 0.7 %copy-start.3 = (s32[4]{0:T(128)S(1)}, s32[4]{0:T(128)}, u32[]{:S(2)}) copy-start(s32[4]{0:T(128)} %dest_ref.1) | copy-start | bytes 52
  4.4 0.7 %copy-start.4 = (s32[8]{0:T(128)S(1)}, s32[8]{0:T(128)}, u32[]{:S(2)}) copy-start(s32[8]{0:T(128)} %place_ref.1) | copy-start | bytes 100

commit v2 on v1

--- a/solution.py
+++ b/solution.py
@@ -11,13 +11,14 @@
 HD = 128
 EPSILON = 1e-06
 ROPE_BASE = 1000000.0
-LOOKAHEAD = 3
+LOOKAHEAD = 8
 MESH = pl.DeviceIdType.MESH
+GAP = 2
 Y, UP, DOWN = 0, 1, 2
 
 
 def kernel(
-    team, chunks, page_len, page_count, slots,
+    team, chunks, crossed, page_len, page_count, slots,
     request_ref, dest_ref, slot_ref, place_ref,
     hidden_hbm, gain_hbm, weight_hbm, bias_hbm,
     out_ref,
@@ -110,6 +111,38 @@
         for copy in copies(c, block, Y):
             copy.wait_recv()
 
+    both = ((UP, has_up), (DOWN, has_down))
+
+    def hops(c):
+        found = []
+        for step in range(1, line):
+            low, high = z >= step, z + step < line
+            if c < crossed:
+                found += [
+                    (step, low, me - 2 * step, both[:1]),
+                    (step, high, me + 2 * step, both[1:]),
+                    (step + 1, low, peer[Y] - 2 * step, both[:1]),
+                    (step + 1, high, peer[Y] + 2 * step, both[1:]),
+                ]
+            else:
+                found += [
+                    (step, low, me - 2 * step, ((Y, None),) + both[:1]),
+                    (step, high, me + 2 * step, ((Y, None),) + both[1:]),
+                ]
+        if c < crossed:
+            found.append((1, None, peer[Y], both))
+        return found
+
+    def guarded(cond, act):
+        if cond is None:
+            act()
+        else:
+            pl.when(cond)(act)
+
+    def onward(act, c, block, ways):
+        for way, cond in ways:
+            guarded(cond, functools.partial(act, c, block, way))
+
     def send_own(c):
         span = slice(c * depth, (c + 1) * depth)
         normed = [
@@ -117,24 +150,11 @@
             for layer in range(layers)
         ]
         rows[c, me] = jnp.concatenate(normed, axis=0).astype(jnp.bfloat16)
-        send(c, me, Y)
-        pl.when(has_up)(lambda: send(c, me, UP))
-        pl.when(has_down)(lambda: send(c, me, DOWN))
-
-    def forward(c, step):
-        low, high = me - 2 * step, me + 2 * step
-
-        @pl.when(z >= step)
-        def _():
-            receive(c, low)
-            send(c, low, Y)
-            pl.when(has_up)(lambda: send(c, low, UP))
-
-        @pl.when(z + step < line)
-        def _():
-            receive(c, high)
-            send(c, high, Y)
-            pl.when(has_down)(lambda: send(c, high, DOWN))
+        onward(send, c, me, ((Y, None),) + both)
+
+    def forward(c, block, ways):
+        receive(c, block)
+        onward(send, c, block, ways)
 
     tokens = team * row_count
     places = page_len * slots
@@ -165,41 +185,50 @@
         hit = (code == inst * slots + spot % slots) & (token % page_len == spot // slots)
         pick[side] = jnp.where(hit, 1.0, 0.0).T.astype(jnp.bfloat16)
 
-    def multiply(c):
+    def multiply(c, fresh):
         block = rows[c].reshape(team * layers * row_count, depth)
         for layer in range(layers):
             part = lax.dot_general(
                 block, weight[layer, :, c * depth:(c + 1) * depth],
                 (((1,), (1,)), ((), ())), preferred_element_type=jnp.float32,
             )
-            if c == 0:
+            if fresh:
                 total[layer, :, :width] = part
             else:
                 total[layer, :, :width] += part
 
     if wide != width:
         total[...] = jnp.zeros_like(total)
-    for c in range(min(LOOKAHEAD, chunks)):
-        send_own(c)
-    for wave in range(chunks + line):
-        if wave + LOOKAHEAD < chunks:
-            send_own(wave + LOOKAHEAD)
-        for step in range(1, line):
-            if 0 <= wave - step < chunks:
-                forward(wave - step, step)
-        c = wave - line
-        if 0 <= c < chunks:
+    gap = GAP or chunks
+    events = []
+    for c in range(chunks):
+        events.append((max(0, c - LOOKAHEAD), 0, len(events), functools.partial(send_own, c)))
+        for stage, cond, block, ways in hops(c):
+            act = functools.partial(guarded, cond, functools.partial(forward, c, block, ways))
+            events.append((c + gap * stage, 1, len(events), act))
+
+    first = crossed if crossed < chunks else 0
+
+    def finish(c):
+        if c >= crossed:
             for far in range(line):
                 receive(c, 2 * far + 1 - y)
-            if c == 0:
-                pair_code.start()
-                loads[2].wait()
-                loads[3].wait()
-                tables()
-                picks(0, meta)
-            multiply(c)
-    pair_code.wait_recv()
-    picks(1, far_code)
+        if c == first:
+            loads[2].wait()
+            loads[3].wait()
+        multiply(c, c == first)
+        if c == 0:
+            pair_code.start()
+            tables()
+            picks(0, meta)
+        if c == min(1, chunks - 1):
+            pair_code.wait_recv()
+            picks(1, far_code)
+
+    for c in range(chunks):
+        events.append((max(c + gap * line, c + gap * (line + 1) if c < crossed else 0), 2, len(events), functools.partial(finish, c)))
+    for event in sorted(events, key=lambda e: e[:3]):
+        event[3]()
 
     lane = lax.broadcasted_iota(jnp.int32, (1, 128), 1)
     for layer in range(layers):
@@ -245,21 +274,9 @@
     pair_code.wait_send()
     swap.wait_send()
     for c in range(chunks):
-        sent(c, me, Y)
-        pl.when(has_up)(functools.partial(sent, c, me, UP))
-        pl.when(has_down)(functools.partial(sent, c, me, DOWN))
-        for step in range(1, line):
-            low, high = me - 2 * step, me + 2 * step
-
-            @pl.when(z >= step)
-            def _():
-                sent(c, low, Y)
-                pl.when(has_up)(functools.partial(sent, c, low, UP))
-
-            @pl.when(z + step < line)
-            def _():
-                sent(c, high, Y)
-                pl.when(has_down)(functools.partial(sent, c, high, DOWN))
+        onward(sent, c, me, ((Y, None),) + both)
+        for _, cond, block, ways in hops(c):
+            guarded(cond, functools.partial(onward, sent, c, block, ways))
 
 
 def body(hidden, norm_gain, kv_weight, kv_bias, block_request, request_dest, block_slot, positions):
@@ -271,7 +288,7 @@
     team = lax.axis_size("tp")
     slots = inst_count * team * page_count
     wide = -(-width // 128) * 128
-    chunks = max(1, 64 // team)
+    chunks = max(1, 32 // team)
     depth = model_dim // chunks
     tokens = team * row_count
     line = team // 2
@@ -283,7 +300,7 @@
     anywhere = pl.BlockSpec(memory_space=pl.ANY)
     dma = pltpu.SemaphoreType.DMA
     out = pl.pallas_call(
-        functools.partial(kernel, team, chunks, page_len, page_count, slots),
+        functools.partial(kernel, team, chunks, chunks // 8, page_len, page_count, slots),
         out_shape=jax.ShapeDtypeStruct(shape, jnp.bfloat16),
         in_specs=[smem] * 4 + [anywhere] * 4,
         out_specs=pl.BlockSpec(memory_space=pltpu.VMEM),
@@ -309,7 +326,7 @@
             dma((2,)),
         ],
         compiler_params=pltpu.CompilerParams(
-            collective_id=0, has_side_effects=True, vmem_limit_bytes=48 * 1024 * 1024
+            collective_id=0, has_side_effects=True, vmem_limit_bytes=62 * 1024 * 1024
         ),
         cost_estimate=pl.CostEstimate(
             flops=4 * layers * tokens * width * model_dim,

time: 44.2 us -> 36.1 us (0.82)
  Pallas kernels: 38.1 us -> 32.9 us
  local copies, waits for them, and re-layouts: 4.43 us -> 1.57 us
    pallas_call x1, Pallas kernels: 38.1 us -> 32.9 us  [body(): pl.pallas_call(functools.partial(kernel, team, chunks, chunks // 8, page_...]
    unnamed x11 -> x1, local copies, waits for them, and re-layouts: 4.43 us -> 1.57 us
where the time goes in v2:
time: 36.1 us; the launch traced here: 35.8 us
  Pallas kernels  32.9 us (91%)
  local copies, waits for them, and re-layouts  1.57 us (4%)
  between operations  1.3 us (4%)
    pallas_call x1, Pallas kernels, body(): pl.pallas_call(functools.partial(kernel, team, chunks, chunks // 8, page_...  32.9 us
    unnamed x1, local copies, waits for them, and re-layouts  1.57 us

profile of v2, /device:TPU:0, one launch (start us, length us, event | category | flops | bytes accessed | tf_op | source)
XLA Modules:
  0.0 35.8 jit_solution(18150239175943333076)
XLA Ops:
  1.3 32.9 %restore.1 = bf16[2,16,2048]{2,1,0:T(8,128)(2,1)} custom-call(s32[1]{0:T(128)S(6)} %copy.11.request_ref, s32[4]{0:T(128)} %dest_ref.1, s32[1]{0:T(128)S(6)} %copy.12.slot_ref, s32[8]{0:T(128)} %place_ref.1, bf16[2,8,8192]{2,1,0:T(8,128)(2,1)} %hidden_hbm.1, f32[2,8192]{1,0:T(2,128)} %gain_hbm.1, bf16[2,256,8192]{2,1,0:T(8,128)(2,1)} %weight_hbm.1, ...), custom_call_target="tpu_custom_call" | custom-call | flops 1073741824 | bytes 8388608 | tf_op jit(solution)/shard_map/restore/pallas_call | solution.py:302
  34.2 1.6 %copy.13 = bf16[2,16,1,2048]{3,1,2,0:T(8,128)(2,1)} copy(bf16[2,16,1,2048]{3,1,2,0:T(8,128)(2,1)} %bitcast.3) | data formatting | bytes 262144

commit v3 on v2

--- a/solution.py
+++ b/solution.py
@@ -126,8 +126,8 @@
                 ]
             else:
                 found += [
-                    (step, low, me - 2 * step, ((Y, None),) + both[:1]),
-                    (step, high, me + 2 * step, ((Y, None),) + both[1:]),
+                    (step, low, me - 2 * step, both[:1] + ((Y, None),)),
+                    (step, high, me + 2 * step, both[1:] + ((Y, None),)),
                 ]
         if c < crossed:
             found.append((1, None, peer[Y], both))
@@ -150,7 +150,7 @@
             for layer in range(layers)
         ]
         rows[c, me] = jnp.concatenate(normed, axis=0).astype(jnp.bfloat16)
-        onward(send, c, me, ((Y, None),) + both)
+        onward(send, c, me, both + ((Y, None),))
 
     def forward(c, block, ways):
         receive(c, block)

time: 36.1 us -> 36.1 us (level)
  no operation moved by 1% of the time
where the time goes in v3:
time: 36.1 us; the launch traced here: 35.8 us
  Pallas kernels  32.9 us (91%)
  local copies, waits for them, and re-layouts  1.57 us (4%)
  between operations  1.3 us (4%)
    pallas_call x1, Pallas kernels, body(): pl.pallas_call(functools.partial(kernel, team, chunks, chunks // 8, page_...  32.9 us
    unnamed x1, local copies, waits for them, and re-layouts  1.57 us

profile of v3, /device:TPU:0, one launch (start us, length us, event | category | flops | bytes accessed | tf_op | source)
XLA Modules:
  0.0 35.8 jit_solution(7182800561222977637)
XLA Ops:
  1.3 32.9 %restore.1 = bf16[2,16,2048]{2,1,0:T(8,128)(2,1)} custom-call(s32[1]{0:T(128)S(6)} %copy.11.request_ref, s32[4]{0:T(128)} %dest_ref.1, s32[1]{0:T(128)S(6)} %copy.12.slot_ref, s32[8]{0:T(128)} %place_ref.1, bf16[2,8,8192]{2,1,0:T(8,128)(2,1)} %hidden_hbm.1, f32[2,8192]{1,0:T(2,128)} %gain_hbm.1, bf16[2,256,8192]{2,1,0:T(8,128)(2,1)} %weight_hbm.1, ...), custom_call_target="tpu_custom_call" | custom-call | flops 1073741824 | bytes 8388608 | tf_op jit(solution)/shard_map/restore/pallas_call | solution.py:302
  34.2 1.6 %copy.13 = bf16[2,16,1,2048]{3,1,2,0:T(8,128)(2,1)} copy(bf16[2,16,1,2048]{3,1,2,0:T(8,128)(2,1)} %bitcast.3) | data formatting | bytes 262144
